TPU v7x, 512 devices: a whole 4x4x16 slice. The times are simulated.
512 devices in a mesh: section: 4 (over x), replica: 16 (over z_lo, y), expert: 8 (over z_hi, core).
Axes of the slice: x: 4, y: 4, z: 16 (z_hi: 4, z_lo: 4; z = z_hi * 4 + z_lo), core: 2. Of those that a mesh axis runs over, the one named last changes fastest.
Arguments:
- tokens: bfloat16 [3, 256, 1536], P(None, 'replica'), may hold values from -6 to 6
- attn_gain: float32 [4, 1536], P('section'), may hold values from 0.25 to 1.75
- w_query: bfloat16 [4, 1536, 2048], P('section', None, 'expert'), may hold values from -0.15625 to 0.15625
- w_keyval: bfloat16 [4, 1536, 8, 128], P('section', None, 'expert'), may hold values from -0.15625 to 0.15625
- sinks: float32 [4, 32], P('section', 'expert'), may hold values from -2 to 260
- w_out: bfloat16 [4, 2048, 1536], P('section', 'expert'), may hold values from -0.125 to 0.125
- ffn_gain: float32 [4, 1536], P('section'), may hold values from 0.25 to 1.75
- router: bfloat16 [4, 1536, 16], P('section'), may hold values from -0.15625 to 0.15625
- w_gate_up: bfloat16 [4, 16, 2, 1536, 2048], P('section', 'replica', None, None, 'expert'), may hold values from -0.15625 to 0.15625
- w_down: bfloat16 [4, 16, 2048, 1536], P('section', 'replica', 'expert'), may hold values from -0.125 to 0.125
- kv_pool: bfloat16 [4, 2048, 16, 8, 128], P('section', 'replica', None, 'expert'), may hold values from -6 to 6
- block_table: int32 [256, 8], P('replica'), may hold values from 0 to 127, as said below
- lengths: int32 [256], P('replica'), may hold values from 1 to 128, as said below
- expert_ids: int32 [4, 3, 256, 4], P('section', None, 'replica'), may hold values from 0 to 15, all different within a row; in each aligned block of 16 rows (0 to 15, 16 to 31, ..., all dimensions but the last counted through in order) at most 5 rows name the same one
Outputs:
- layer_out: bfloat16 [4, 3, 256, 1536], P('section', None, 'replica', 'expert')
- fresh_kv: bfloat16 [4, 3, 256, 8, 128], P('section', None, 'replica', 'expert')
Inputs may be any that keep to these rules, and one draw needn't show every extreme that they name: `block_table`: rows 0 to 11 of each replica are its own requests and index its own pool; its last 4 rows are requests taken over from the replica before it (replica 0 from the last one) and index that replica's pool. All blocks named in one pool are different. `lengths`: some request has exactly 128 cached tokens. `expert_ids`: A row names 4 different experts. For each layer and step, at most 5 of one replica's 16 rows name the same expert, and that count is reached.
All inputs are finite; a program needn't handle non-finite values.
Results may differ from a plain program's by a relative error of at most 0.027.
Values may be sent and summed in bfloat16 or wider, within the bound.
A program may use at most 64 MiB of HBM per device.

v0:
```python
import jax
import jax.numpy as jnp
from jax import lax
from jax.sharding import PartitionSpec as P

MIG = 4
EPS = 1e-05
THETA = 150000.0
NEG = -1e30


def shifted(shard, axis, by):
    length = lax.axis_size(axis)
    return lax.ppermute(shard, axis, [(i, (i + by) % length) for i in range(length)])


def shifted_2(value, axis, steps):
    count = lax.axis_size(axis)
    leading, last = (max(0, -steps), min(count, count - steps))
    return lax.ppermute(value, axis, [(source, source + steps) for source in range(leading, last)])


def normed(values, gain):
    wide = values.astype(jnp.float32)
    mean_sq = jnp.mean(wide * wide, axis=-1, keepdims=True)
    return (wide * lax.rsqrt(mean_sq + EPS) * gain).astype(jnp.bfloat16)


def rotated(vectors, places):
    half = vectors.shape[-1] // 2
    freq = THETA ** (-2.0 * jnp.arange(half).astype(jnp.float32) / vectors.shape[-1])
    angle = places.astype(jnp.float32)[:, None] * freq[None, :]
    cosine = jnp.cos(angle)[:, None, :]
    sine = jnp.sin(angle)[:, None, :]
    first = vectors[..., :half]
    second = vectors[..., half:]
    return jnp.concatenate(
        [first * cosine - second * sine, second * cosine + first * sine], axis=-1
    )


def attend(query, cache, live_len, fresh, step_at, sink):
    head_dim = query.shape[-1]
    scale = head_dim ** (-0.5)
    past_keys = cache[..., :head_dim]
    past_vals = cache[..., head_dim:]
    score = (
        jnp.einsum("rkgd,rckd->rkgc", query, past_keys, preferred_element_type=jnp.float32) * scale
    )
    live = jnp.arange(cache.shape[1])[None, :] < live_len[:, None]
    score = jnp.where(live[:, None, None, :], score, NEG)
    new_keys = fresh[..., :head_dim]
    new_vals = fresh[..., head_dim:]
    recent = (
        jnp.einsum("rkgd,srkd->rkgs", query, new_keys, preferred_element_type=jnp.float32) * scale
    )
    seen = jnp.arange(fresh.shape[0]) <= step_at
    recent = jnp.where(seen[None, None, None, :], recent, NEG)
    peak = jnp.maximum(jnp.maximum(jnp.max(score, -1), jnp.max(recent, -1)), sink[None])
    past_w = jnp.exp(score - peak[..., None])
    new_w = jnp.exp(recent - peak[..., None])
    total = jnp.sum(past_w, -1) + jnp.sum(new_w, -1) + jnp.exp(sink[None] - peak)
    past_b = (past_w / total[..., None]).astype(jnp.bfloat16)
    new_b = (new_w / total[..., None]).astype(jnp.bfloat16)
    merged = jnp.einsum("rkgc,rckd->rkgd", past_b, past_vals, preferred_element_type=jnp.float32)
    merged = merged + jnp.einsum(
        "rkgs,srkd->rkgd", new_b, new_vals, preferred_element_type=jnp.float32
    )
    return merged.astype(jnp.bfloat16)


def local(
    tokens,
    attn_gain,
    w_query,
    w_keyval,
    sinks,
    w_out,
    ffn_gain,
    router,
    w_gate_up,
    w_down,
    kv_pool,
    block_table,
    lengths,
    expert_ids,
):
    step_count, row_count, model_width = tokens.shape
    expert_count = router.shape[2]
    kv_local = w_keyval.shape[2]
    pair_width = w_keyval.shape[3]
    head_dim = pair_width // 2
    q_local = sinks.shape[1]
    group = q_local // kv_local
    choose_count = expert_ids.shape[3]
    part_count = lax.axis_size("expert")
    share_width = model_width // part_count
    slot_cap = min(
        row_count, (5 * row_count * choose_count + 4 * expert_count - 1) // (4 * expert_count)
    )
    section_index = lax.axis_index("section")
    lane_index = lax.axis_index("expert")
    section_count = lax.axis_size("section")
    own_pool = kv_pool[0]
    block_count = block_table.shape[1]
    depth = block_count * own_pool.shape[1]
    staying = row_count - MIG
    wanted = shifted(block_table[staying:], "replica", -1)
    leaving = own_pool[wanted.reshape(-1)]
    arrived = shifted(leaving, "replica", 1)
    resident = own_pool[block_table[:staying].reshape(-1)]
    cache = jnp.concatenate([resident, arrived], axis=0).reshape(
        row_count, depth, kv_local, pair_width
    )
    query_weight = w_query[0]
    keyval_weight = w_keyval[0].reshape(model_width, kv_local * pair_width)
    out_weight = w_out[0]
    sink_local = sinks[0].reshape(kv_local, group)
    router_weight = router[0]
    gate_up = w_gate_up[0, 0]
    down_weight = w_down[0, 0]
    expert_range = jnp.arange(expert_count)
    slot_range = jnp.arange(expert_count * slot_cap)
    fresh = jnp.zeros((step_count, row_count, kv_local, pair_width), jnp.bfloat16)
    results = jnp.zeros((step_count, row_count, share_width), jnp.bfloat16)
    incoming = None
    tick_total = step_count + section_count - 1
    for tick_index in range(tick_total):
        offset = tick_index - section_index
        active = (offset >= 0) & (offset < step_count)
        step_at = jnp.clip(offset, 0, step_count - 1)
        first_input = lax.dynamic_index_in_dim(tokens, step_at, 0, keepdims=False)
        if tick_index == 0:
            current = first_input
        else:
            current = jnp.where(section_index == 0, first_input, incoming)
        places = lengths + step_at
        normal_in = normed(current, attn_gain[0])
        query = jnp.dot(normal_in, query_weight, preferred_element_type=jnp.float32).reshape(
            row_count, q_local, head_dim
        )
        query = (
            rotated(query, places)
            .astype(jnp.bfloat16)
            .reshape(row_count, kv_local, group, head_dim)
        )
        keyval = jnp.dot(normal_in, keyval_weight, preferred_element_type=jnp.float32).reshape(
            row_count, kv_local, pair_width
        )
        new_entry = jnp.concatenate(
            [rotated(keyval[..., :head_dim], places), keyval[..., head_dim:]], axis=-1
        ).astype(jnp.bfloat16)
        fresh_now = fresh.at[step_at].set(new_entry)
        attended = attend(query, cache, lengths, fresh_now, step_at, sink_local).reshape(
            row_count, q_local * head_dim
        )
        mixed = lax.psum(
            jnp.dot(attended, out_weight, preferred_element_type=jnp.float32).astype(jnp.bfloat16),
            "expert",
        ).astype(jnp.float32)
        after_attn = (current.astype(jnp.float32) + mixed).astype(jnp.bfloat16)
        mlp_in = normed(after_attn, ffn_gain[0])
        logits = jnp.dot(mlp_in, router_weight, preferred_element_type=jnp.float32)
        chosen = lax.dynamic_index_in_dim(expert_ids[0], step_at, 0, keepdims=False)
        chosen_hot = chosen[:, :, None] == expert_range[None, None, :]
        gates = jax.nn.sigmoid(jnp.sum(jnp.where(chosen_hot, logits[:, None, :], 0.0), -1))
        weight = gates / jnp.sum(gates, -1, keepdims=True)
        flat_hot = chosen_hot.reshape(row_count * choose_count, expert_count).astype(jnp.int32)
        earlier = jnp.cumsum(flat_hot, axis=0) - flat_hot
        slot_of = jnp.sum(earlier * flat_hot, -1)
        target = chosen.reshape(-1) * slot_cap + slot_of
        placing = jnp.any(
            slot_range[:, None, None] == target.reshape(row_count, choose_count)[None], -1
        ).astype(jnp.bfloat16)
        outbound = jnp.dot(placing, mlp_in, preferred_element_type=jnp.float32).astype(jnp.bfloat16)
        outbound = outbound.reshape(expert_count, slot_cap, model_width)
        batch = lax.all_to_all(outbound, "replica", split_axis=0, concat_axis=0, tiled=True)
        source_count = batch.shape[0]
        slot_count = batch.shape[1]
        flat_in = batch.reshape(source_count * slot_count, batch.shape[2])
        gate_part = jnp.dot(flat_in, gate_up[0], preferred_element_type=jnp.float32)
        up_part = jnp.dot(flat_in, gate_up[1], preferred_element_type=jnp.float32)
        hidden = (jax.nn.silu(gate_part) * up_part).astype(jnp.bfloat16)
        partial_out = jnp.dot(hidden, down_weight, preferred_element_type=jnp.float32).reshape(
            source_count, slot_count, model_width
        )
        summed = lax.psum(partial_out.astype(jnp.bfloat16), "expert")
        returned = lax.all_to_all(summed, "replica", split_axis=0, concat_axis=0, tiled=True)
        picked = returned.reshape(expert_count * slot_cap, model_width)[target]
        picked = picked.reshape(row_count, choose_count, model_width).astype(jnp.float32)
        finished = (after_attn.astype(jnp.float32) + jnp.sum(weight[..., None] * picked, 1)).astype(
            jnp.bfloat16
        )
        share_out = lax.dynamic_slice_in_dim(finished, lane_index * share_width, share_width, 1)
        outgoing = finished
        outgoing, share_out, new_entry = (outgoing, share_out, new_entry)
        fresh = jnp.where(active, fresh.at[step_at].set(new_entry), fresh)
        results = jnp.where(active, results.at[step_at].set(share_out), results)
        if tick_index + 1 < tick_total:
            incoming = shifted_2(outgoing, "section", 1)
    return (results[None], fresh[None])


def solution(mesh):
    return jax.shard_map(
        local,
        mesh=mesh,
        in_specs=(
            P(None, "replica", None),
            P("section", None),
            P("section", None, "expert"),
            P("section", None, "expert", None),
            P("section", "expert"),
            P("section", "expert", None),
            P("section", None),
            P("section", None, None),
            P("section", "replica", None, None, "expert"),
            P("section", "replica", "expert", None),
            P("section", "replica", None, "expert", None),
            P("replica", None),
            P("replica"),
            P("section", None, "replica", None),
        ),
        out_specs=(
            P("section", None, "replica", "expert"),
            P("section", None, "replica", "expert", None),
        ),
        check_vma=False,
    )
```

profile of v0, /device:TPU:1, one launch (start us, length us, event | category | flops | bytes accessed | tf_op | source)
XLA Modules:
  0.0 1151.9 jit_solution(12323026308020968581)
XLA Ops:
  8.1 9.5 collective-permute-start
  29.7 1.9 collective-permute-start.1
  32.5 7.0 collective-permute-done.1
  43.5 38.7 %psum.84 = bf16[16,1536]{1,0:T(8,128)(2,1)S(1)} all-reduce(bf16[16,1536]{1,0:T(8,128)(2,1)S(1)} %convolution_convert_fusion.17), channel_id=1, replica_groups=mesh['section'=4,'replica'=16,'expert'=8] {'expert'}, use_global_device_ids=true, to_apply=%region_7.8 | all-reduce | flops 24576 | bytes 98304 | tf_op jit(solution)/shard_map/psum | solution.py:157
  83.4 3.6 all-to-all-start
  87.8 9.2 all-to-all-done
  97.8 1.5 fusion.46
  99.3 1.5 fusion
  102.7 97.5 %all-reduce.7.cloned.1.call-done = bf16[16,5,1536]{2,0,1:T(8,128)(2,1)} async-done(((bf16[16,5,1536]{2,0,1:T(8,128)(2,1)}), bf16[16,5,1536]{2,0,1:T(8,128)(2,1)}) %all-reduce.7.cloned.1.call-update) | async-done | bytes 245776 | tf_op jit(solution)/shard_map/psum | solution.py:187
  200.2 1.8 copy.261
  202.1 6.5 all-to-all-start.1
  211.7 9.4 all-to-all-done.1
  221.2 1.5 gather_fusion.2
  225.7 3.7 collective-permute-start.2
  236.0 35.0 %psum.86 = bf16[16,1536]{1,0:T(8,128)(2,1)S(1)} all-reduce(bf16[16,1536]{1,0:T(8,128)(2,1)S(1)} %convolution_convert_fusion.16), channel_id=1, replica_groups=mesh['section'=4,'replica'=16,'expert'=8] {'expert'}, use_global_device_ids=true, to_apply=%region_23.24 | all-reduce | flops 24576 | bytes 98304 | tf_op jit(solution)/shard_map/psum | solution.py:157
  273.0 3.9 all-to-all-start.2
  277.7 11.1 all-to-all-done.2
  289.5 1.5 fusion.44
  291.1 1.5 fusion.1
  294.4 93.6 %all-reduce.9.cloned.1.call-done = bf16[16,5,1536]{2,0,1:T(8,128)(2,1)} async-done(((bf16[16,5,1536]{2,0,1:T(8,128)(2,1)}), bf16[16,5,1536]{2,0,1:T(8,128)(2,1)}) %all-reduce.9.cloned.1.call-update) | async-done | bytes 245776 | tf_op jit(solution)/shard_map/psum | solution.py:187
  388.0 1.8 copy.272
  389.8 6.5 all-to-all-start.3
  399.5 9.4 all-to-all-done.3
  408.9 1.5 gather_fusion.3
  413.5 3.3 collective-permute-start.3
  421.9 35.0 %psum.88 = bf16[16,1536]{1,0:T(8,128)(2,1)S(1)} all-reduce(bf16[16,1536]{1,0:T(8,128)(2,1)S(1)} %convolution_convert_fusion.15), channel_id=1, replica_groups=mesh['section'=4,'replica'=16,'expert'=8] {'expert'}, use_global_device_ids=true, to_apply=%region_39.40 | all-reduce | flops 24576 | bytes 98304 | tf_op jit(solution)/shard_map/psum | solution.py:157
  458.2 3.9 all-to-all-start.4
  462.7 11.3 all-to-all-done.4
  474.8 1.5 fusion.42
  476.3 1.5 fusion.2
  479.2 93.0 %all-reduce.11.cloned.1.call-done = bf16[16,5,1536]{2,0,1:T(8,128)(2,1)} async-done(((bf16[16,5,1536]{2,0,1:T(8,128)(2,1)}), bf16[16,5,1536]{2,0,1:T(8,128)(2,1)}) %all-reduce.11.cloned.1.call-update) | async-done | bytes 245776 | tf_op jit(solution)/shard_map/psum | solution.py:187
  572.2 1.8 copy.283
  574.1 6.5 all-to-all-start.5
  584.3 8.8 all-to-all-done.5
  593.1 1.5 gather_fusion.4
  597.7 3.1 collective-permute-start.4
  606.1 35.0 %psum.90 = bf16[16,1536]{1,0:T(8,128)(2,1)S(1)} all-reduce(bf16[16,1536]{1,0:T(8,128)(2,1)S(1)} %convolution_convert_fusion.14), channel_id=1, replica_groups=mesh['section'=4,'replica'=16,'expert'=8] {'expert'}, use_global_device_ids=true, to_apply=%region_55.56 | all-reduce | flops 24576 | bytes 98304 | tf_op jit(solution)/shard_map/psum | solution.py:157
  642.4 3.9 all-to-all-start.6
  647.0 11.1 all-to-all-done.6
  658.9 1.5 fusion.40
  660.4 1.5 fusion.3
  663.8 92.7 %all-reduce.13.cloned.1.call-done = bf16[16,5,1536]{2,0,1:T(8,128)(2,1)} async-done(((bf16[16,5,1536]{2,0,1:T(8,128)(2,1)}), bf16[16,5,1536]{2,0,1:T(8,128)(2,1)}) %all-reduce.13.cloned.1.call-update) | async-done | bytes 245776 | tf_op jit(solution)/shard_map/psum | solution.py:187
  756.5 1.8 copy.294
  758.3 6.5 all-to-all-start.7
  768.0 9.4 all-to-all-done.7
  777.4 1.5 gather_fusion.5
  782.0 3.1 collective-permute-start.5
  790.4 35.0 %psum.92 = bf16[16,1536]{1,0:T(8,128)(2,1)S(1)} all-reduce(bf16[16,1536]{1,0:T(8,128)(2,1)S(1)} %convolution_convert_fusion.13), channel_id=1, replica_groups=mesh['section'=4,'replica'=16,'expert'=8] {'expert'}, use_global_device_ids=true, to_apply=%region_71.72 | all-reduce | flops 24576 | bytes 98304 | tf_op jit(solution)/shard_map/psum | solution.py:157
  826.7 3.9 all-to-all-start.8
  831.4 11.0 all-to-all-done.8
  843.2 1.5 fusion.38
  844.7 1.5 fusion.4
  848.2 92.5 %all-reduce.15.cloned.1.call-done = bf16[16,5,1536]{2,0,1:T(8,128)(2,1)} async-done(((bf16[16,5,1536]{2,0,1:T(8,128)(2,1)}), bf16[16,5,1536]{2,0,1:T(8,128)(2,1)}) %all-reduce.15.cloned.1.call-update) | async-done | bytes 245776 | tf_op jit(solution)/shard_map/psum | solution.py:187
  940.7 1.8 copy.305
  942.5 6.5 all-to-all-start.9
  953.5 8.1 all-to-all-done.9
  966.2 3.1 collective-permute-start.6
  974.5 35.1 %psum.94 = bf16[16,1536]{1,0:T(8,128)(2,1)S(1)} all-reduce(bf16[16,1536]{1,0:T(8,128)(2,1)S(1)} %convolution_convert_fusion.12), channel_id=1, replica_groups=mesh['section'=4,'replica'=16,'expert'=8] {'expert'}, use_global_device_ids=true, to_apply=%region_87.88 | all-reduce | flops 24576 | bytes 98304 | tf_op jit(solution)/shard_map/psum | solution.py:157
  1010.8 3.9 all-to-all-start.10
  1020.6 6.0 all-to-all-done.10
  1030.4 91.2 %all-reduce.17.cloned.1.call-done = bf16[16,5,1536]{2,0,1:T(8,128)(2,1)} async-done(((bf16[16,5,1536]{2,0,1:T(8,128)(2,1)}), bf16[16,5,1536]{2,0,1:T(8,128)(2,1)}) %all-reduce.17.cloned.1.call-update) | async-done | bytes 245776 | tf_op jit(solution)/shard_map/psum | solution.py:187
  1121.6 1.8 copy.316
  1123.4 6.5 all-to-all-start.11
  1131.1 11.3 all-to-all-done.11
  (593 shorter events, 116.5 us)
Async XLA Ops:
  7.2 93.7 %copy-start = (bf16[1,1,256,1536]{3,2,1,0:T(8,128)(2,1)S(1)}, bf16[1,1,256,1536]{3,2,1,0:T(8,128)(2,1)}, u32[]{:S(2)}) copy-start(bf16[1,1,256,1536]{3,2,1,0:T(8,128)(2,1)} %param.59) | copy-start | bytes 2359300
  8.1 20.6 %collective-permute-start = (s32[4,8]{0,1:T(8,128)S(1)}, s32[4,8]{0,1:T(8,128)S(1)}, u32[]{:S(2)}, u32[]{:S(2)}) collective-permute-start(s32[4,8]{0,1:T(8,128)S(1)} %slice.535), channel_id=1, source_target_pairs={{0,120},{8,0},{16,8},{24,16},{32,24},{40,32},{48,40},{56,48},{64,5... | collective-permute-start | bytes 392 | tf_op jit(solution)/shard_map/ppermute | solution.py:14
  21.1 66.6 %copy-start.52 = (s32[1,1,16,4]{2,3,1,0:T(4,128)}, s32[1,1,16,4]{2,3,1,0:T(4,128)S(1)}, u32[]{:S(2)}) copy-start(s32[1,1,16,4]{2,3,1,0:T(4,128)S(1)} %get-tuple-element.289) | copy-start | bytes 772
  26.7 182.5 %copy-start.16 = (bf16[3,16,1,128]{3,1,2,0:T(8,128)(2,1)}, bf16[3,16,1,128]{3,1,2,0:T(8,128)(2,1)S(1)}, u32[]{:S(2)}) copy-start(bf16[3,16,1,128]{3,1,2,0:T(8,128)(2,1)S(1)} %constant_dynamic-update-slice_fusion.11) | copy-start | bytes 36868
  29.7 9.7 collective-permute-start.1
  82.3 127.5 %copy-start.15 = (bf16[16,1536]{1,0:T(8,128)(2,1)}, bf16[16,1536]{1,0:T(8,128)(2,1)S(1)}, u32[]{:S(2)}) copy-start(bf16[16,1536]{1,0:T(8,128)(2,1)S(1)} %get-tuple-element.245) | copy-start | bytes 147460
  83.4 13.5 %all-to-all-start = ((bf16[16,5,1536]{2,1,0:T(8,128)(2,1)}), bf16[16,5,1536]{2,1,0:T(8,128)(2,1)S(1)}, u32[]{:S(2)}, u32[]{:S(2)}) async-start(bf16[16,5,1536]{2,1,0:T(8,128)(2,1)} %reshape.2989), calls=%async_computation | async-start | bytes 786432 | tf_op jit(solution)/shard_map/all_to_all | solution.py:177
  87.0 113.2 %all-reduce.7.cloned.1.call-start = ((), (), s32[]{:S(2)}) async-start(), calls=%async_computation.12 | async-start | bytes 491520 | tf_op jit(solution)/shard_map/psum | solution.py:187
  202.1 19.0 %all-to-all-start.1 = ((bf16[16,5,1536]{2,1,0:T(8,128)(2,1)}), bf16[16,5,1536]{2,1,0:T(8,128)(2,1)S(1)}, u32[]{:S(2)}, u32[]{:S(2)}) async-start(bf16[16,5,1536]{2,1,0:T(8,128)(2,1)} %copy.261), calls=%async_computation.1 | async-start | bytes 786432 | tf_op jit(solution)/shard_map/all_to_all | solution.py:188
  225.7 4.6 collective-permute-start.2
  234.6 38.3 %copy-start.18 = (bf16[3,16,1,128]{3,1,2,0:T(8,128)(2,1)}, bf16[3,16,1,128]{3,1,2,0:T(8,128)(2,1)S(1)}, u32[]{:S(2)}) copy-start(bf16[3,16,1,128]{3,1,2,0:T(8,128)(2,1)S(1)} %constant_dynamic-update-slice_fusion.9) | copy-start | bytes 36868
  235.5 41.4 %copy-start.69 = (s32[1,1,16,4]{2,3,1,0:T(4,128)S(1)}, s32[1,1,16,4]{2,3,1,0:T(4,128)}, u32[]{:S(2)}) copy-start(s32[1,1,16,4]{2,3,1,0:T(4,128)} %get-tuple-element.288) | copy-start | bytes 772
  235.5 41.6 %copy-start.50 = (s32[1,1,16,4]{2,3,1,0:T(4,128)S(1)}, s32[1,1,16,4]{2,3,1,0:T(4,128)}, u32[]{:S(2)}) copy-start(s32[1,1,16,4]{2,3,1,0:T(4,128)} %get-tuple-element.287) | copy-start | bytes 772
  235.7 41.9 %copy-start.86 = (s32[64]{0:T(128)S(1)}, s32[64]{0:T(128)}, u32[]{:S(2)}) copy-start(s32[64]{0:T(128)} %copy-done.85) | copy-start | bytes 772
  271.1 127.2 %copy-start.13 = (bf16[16,1536]{1,0:T(8,128)(2,1)}, bf16[16,1536]{1,0:T(8,128)(2,1)S(1)}, u32[]{:S(2)}) copy-start(bf16[16,1536]{1,0:T(8,128)(2,1)S(1)} %get-tuple-element.239) | copy-start | bytes 147460
  273.0 15.8 %all-to-all-start.2 = ((bf16[16,5,1536]{2,1,0:T(8,128)(2,1)}), bf16[16,5,1536]{2,1,0:T(8,128)(2,1)S(1)}, u32[]{:S(2)}, u32[]{:S(2)}) async-start(bf16[16,5,1536]{2,1,0:T(8,128)(2,1)} %reshape.2996), calls=%async_computation.2 | async-start | bytes 786432 | tf_op jit(solution)/shard_map/all_to_all | solution.py:177
  276.8 111.1 %all-reduce.9.cloned.1.call-start = ((), (), s32[]{:S(2)}) async-start(), calls=%async_computation.13 | async-start | bytes 491520 | tf_op jit(solution)/shard_map/psum | solution.py:187
  292.6 104.3 %copy-start.83 = (s32[4]{0:T(128)S(1)}, s32[4]{0:T(128)}, u32[]{:S(2)}) copy-start(s32[4]{0:T(128)} %constant.446.clone.1) | copy-start | bytes 52
  292.6 105.8 %copy-start.104 = (bf16[1,1536,16]{1,2,0:T(8,128)(2,1)S(1)}, bf16[1,1536,16]{1,2,0:T(8,128)(2,1)}, u32[]{:S(2)}) copy-start(bf16[1,1536,16]{1,2,0:T(8,128)(2,1)} %param.57) | copy-start | bytes 147460
  292.6 105.9 %copy-start.53 = (s32[1,1,16,4]{2,3,1,0:T(4,128)S(1)}, s32[1,1,16,4]{2,3,1,0:T(4,128)}, u32[]{:S(2)}) copy-start(s32[1,1,16,4]{2,3,1,0:T(4,128)} %copy-done.52) | copy-start | bytes 772
  389.8 19.0 %all-to-all-start.3 = ((bf16[16,5,1536]{2,1,0:T(8,128)(2,1)}), bf16[16,5,1536]{2,1,0:T(8,128)(2,1)S(1)}, u32[]{:S(2)}, u32[]{:S(2)}) async-start(bf16[16,5,1536]{2,1,0:T(8,128)(2,1)} %copy.272), calls=%async_computation.3 | async-start | bytes 786432 | tf_op jit(solution)/shard_map/all_to_all | solution.py:188
  413.5 4.6 collective-permute-start.3
  419.3 37.8 %copy-start.63 = (pred[80,16]{0,1:T(8,128)(4,1)S(1)}, pred[80,16]{0,1:T(8,128)(4,1)}, u32[]{:S(2)}) copy-start(pred[80,16]{0,1:T(8,128)(4,1)} %fusion.164) | copy-start | bytes 3844
  421.4 40.8 %copy-start.68 = (s32[1,1,16,4]{2,3,1,0:T(4,128)S(1)}, s32[1,1,16,4]{2,3,1,0:T(4,128)}, u32[]{:S(2)}) copy-start(s32[1,1,16,4]{2,3,1,0:T(4,128)} %get-tuple-element.286) | copy-start | bytes 772
  421.4 40.9 %copy-start.48 = (s32[1,1,16,4]{2,3,1,0:T(4,128)S(1)}, s32[1,1,16,4]{2,3,1,0:T(4,128)}, u32[]{:S(2)}) copy-start(s32[1,1,16,4]{2,3,1,0:T(4,128)} %get-tuple-element.285) | copy-start | bytes 772
  421.6 41.1 %copy-start.90 = (s32[64]{0:T(128)S(1)}, s32[64]{0:T(128)}, u32[]{:S(2)}) copy-start(s32[64]{0:T(128)} %copy-done.89) | copy-start | bytes 772
  457.0 125.3 %copy-start.14 = (bf16[16,1536]{1,0:T(8,128)(2,1)}, bf16[16,1536]{1,0:T(8,128)(2,1)S(1)}, u32[]{:S(2)}) copy-start(bf16[16,1536]{1,0:T(8,128)(2,1)S(1)} %get-tuple-element.233) | copy-start | bytes 147460
  458.2 15.8 %all-to-all-start.4 = ((bf16[16,5,1536]{2,1,0:T(8,128)(2,1)}), bf16[16,5,1536]{2,1,0:T(8,128)(2,1)S(1)}, u32[]{:S(2)}, u32[]{:S(2)}) async-start(bf16[16,5,1536]{2,1,0:T(8,128)(2,1)} %reshape.3004), calls=%async_computation.4 | async-start | bytes 786432 | tf_op jit(solution)/shard_map/all_to_all | solution.py:177
  462.1 110.1 %all-reduce.11.cloned.1.call-start = ((), (), s32[]{:S(2)}) async-start(), calls=%async_computation.14 | async-start | bytes 491520 | tf_op jit(solution)/shard_map/psum | solution.py:187
  477.8 105.5 %copy-start.51 = (s32[1,1,16,4]{2,3,1,0:T(4,128)S(1)}, s32[1,1,16,4]{2,3,1,0:T(4,128)}, u32[]{:S(2)}) copy-start(s32[1,1,16,4]{2,3,1,0:T(4,128)} %get-tuple-element.287) | copy-start | bytes 772
  479.0 105.2 %copy-start.93 = (s32[64]{0:T(128)}, s32[64]{0:T(128)S(1)}, u32[]{:S(2)}) copy-start(s32[64]{0:T(128)S(1)} %select_reduce_fusion.4) | copy-start | bytes 772
  574.1 19.0 %all-to-all-start.5 = ((bf16[16,5,1536]{2,1,0:T(8,128)(2,1)}), bf16[16,5,1536]{2,1,0:T(8,128)(2,1)S(1)}, u32[]{:S(2)}, u32[]{:S(2)}) async-start(bf16[16,5,1536]{2,1,0:T(8,128)(2,1)} %copy.283), calls=%async_computation.5 | async-start | bytes 786432 | tf_op jit(solution)/shard_map/all_to_all | solution.py:188
  597.7 4.6 collective-permute-start.4
  605.5 40.8 %copy-start.67 = (s32[1,1,16,4]{2,3,1,0:T(4,128)S(1)}, s32[1,1,16,4]{2,3,1,0:T(4,128)}, u32[]{:S(2)}) copy-start(s32[1,1,16,4]{2,3,1,0:T(4,128)} %get-tuple-element.284) | copy-start | bytes 772
  605.5 40.9 %copy-start.46 = (s32[1,1,16,4]{2,3,1,0:T(4,128)S(1)}, s32[1,1,16,4]{2,3,1,0:T(4,128)}, u32[]{:S(2)}) copy-start(s32[1,1,16,4]{2,3,1,0:T(4,128)} %get-tuple-element.293) | copy-start | bytes 772
  605.8 41.3 %copy-start.94 = (s32[64]{0:T(128)S(1)}, s32[64]{0:T(128)}, u32[]{:S(2)}) copy-start(s32[64]{0:T(128)} %copy-done.93) | copy-start | bytes 772
  641.2 125.7 %copy-start.12 = (bf16[16,1536]{1,0:T(8,128)(2,1)}, bf16[16,1536]{1,0:T(8,128)(2,1)S(1)}, u32[]{:S(2)}) copy-start(bf16[16,1536]{1,0:T(8,128)(2,1)S(1)} %get-tuple-element.227) | copy-start | bytes 147460
  642.4 15.8 %all-to-all-start.6 = ((bf16[16,5,1536]{2,1,0:T(8,128)(2,1)}), bf16[16,5,1536]{2,1,0:T(8,128)(2,1)S(1)}, u32[]{:S(2)}, u32[]{:S(2)}) async-start(bf16[16,5,1536]{2,1,0:T(8,128)(2,1)} %reshape.3012), calls=%async_computation.6 | async-start | bytes 786432 | tf_op jit(solution)/shard_map/all_to_all | solution.py:177
  646.2 110.2 %all-reduce.13.cloned.1.call-start = ((), (), s32[]{:S(2)}) async-start(), calls=%async_computation.15 | async-start | bytes 491520 | tf_op jit(solution)/shard_map/psum | solution.py:187
  662.0 103.5 %copy-start.84 = (s32[4]{0:T(128)S(1)}, s32[4]{0:T(128)}, u32[]{:S(2)}) copy-start(s32[4]{0:T(128)} %constant.446.clone.1) | copy-start | bytes 52
  662.0 104.9 %copy-start.105 = (bf16[1,1536,16]{1,2,0:T(8,128)(2,1)S(1)}, bf16[1,1536,16]{1,2,0:T(8,128)(2,1)}, u32[]{:S(2)}) copy-start(bf16[1,1536,16]{1,2,0:T(8,128)(2,1)} %param.57) | copy-start | bytes 147460
  662.0 105.0 %copy-start.49 = (s32[1,1,16,4]{2,3,1,0:T(4,128)S(1)}, s32[1,1,16,4]{2,3,1,0:T(4,128)}, u32[]{:S(2)}) copy-start(s32[1,1,16,4]{2,3,1,0:T(4,128)} %get-tuple-element.285) | copy-start | bytes 772
  758.3 19.0 %all-to-all-start.7 = ((bf16[16,5,1536]{2,1,0:T(8,128)(2,1)}), bf16[16,5,1536]{2,1,0:T(8,128)(2,1)S(1)}, u32[]{:S(2)}, u32[]{:S(2)}) async-start(bf16[16,5,1536]{2,1,0:T(8,128)(2,1)} %copy.294), calls=%async_computation.7 | async-start | bytes 786432 | tf_op jit(solution)/shard_map/all_to_all | solution.py:188
  782.0 4.6 collective-permute-start.5
  789.8 41.0 %copy-start.66 = (s32[1,1,16,4]{2,3,1,0:T(4,128)S(1)}, s32[1,1,16,4]{2,3,1,0:T(4,128)}, u32[]{:S(2)}) copy-start(s32[1,1,16,4]{2,3,1,0:T(4,128)} %get-tuple-element.292) | copy-start | bytes 772
  789.8 41.2 %copy-start.44 = (s32[1,1,16,4]{2,3,1,0:T(4,128)S(1)}, s32[1,1,16,4]{2,3,1,0:T(4,128)}, u32[]{:S(2)}) copy-start(s32[1,1,16,4]{2,3,1,0:T(4,128)} %get-tuple-element.215) | copy-start | bytes 772
  790.1 41.3 %copy-start.88 = (s32[64]{0:T(128)S(1)}, s32[64]{0:T(128)}, u32[]{:S(2)}) copy-start(s32[64]{0:T(128)} %copy-done.87) | copy-start | bytes 772
  825.5 126.1 %copy-start.11 = (bf16[16,1536]{1,0:T(8,128)(2,1)}, bf16[16,1536]{1,0:T(8,128)(2,1)S(1)}, u32[]{:S(2)}) copy-start(bf16[16,1536]{1,0:T(8,128)(2,1)S(1)} %get-tuple-element.221) | copy-start | bytes 147460
  826.7 15.8 %all-to-all-start.8 = ((bf16[16,5,1536]{2,1,0:T(8,128)(2,1)}), bf16[16,5,1536]{2,1,0:T(8,128)(2,1)S(1)}, u32[]{:S(2)}, u32[]{:S(2)}) async-start(bf16[16,5,1536]{2,1,0:T(8,128)(2,1)} %reshape.3020), calls=%async_computation.8 | async-start | bytes 786432 | tf_op jit(solution)/shard_map/all_to_all | solution.py:177
  830.5 110.1 %all-reduce.15.cloned.1.call-start = ((), (), s32[]{:S(2)}) async-start(), calls=%async_computation.16 | async-start | bytes 491520 | tf_op jit(solution)/shard_map/psum | solution.py:187
  846.3 103.3 %copy-start.65 = (s32[1,1,16,4]{2,3,1,0:T(4,128)S(1)}, s32[1,1,16,4]{2,3,1,0:T(4,128)}, u32[]{:S(2)}) copy-start(s32[1,1,16,4]{2,3,1,0:T(4,128)} %get-tuple-element.214) | copy-start | bytes 772
  846.3 106.3 %copy-start.47 = (s32[1,1,16,4]{2,3,1,0:T(4,128)S(1)}, s32[1,1,16,4]{2,3,1,0:T(4,128)}, u32[]{:S(2)}) copy-start(s32[1,1,16,4]{2,3,1,0:T(4,128)} %get-tuple-element.293) | copy-start | bytes 772
  942.5 19.0 %all-to-all-start.9 = ((bf16[16,5,1536]{2,1,0:T(8,128)(2,1)}), bf16[16,5,1536]{2,1,0:T(8,128)(2,1)S(1)}, u32[]{:S(2)}, u32[]{:S(2)}) async-start(bf16[16,5,1536]{2,1,0:T(8,128)(2,1)} %copy.305), calls=%async_computation.9 | async-start | bytes 786432 | tf_op jit(solution)/shard_map/all_to_all | solution.py:188
  966.2 4.6 collective-permute-start.6
  971.9 37.8 %copy-start.61 = (pred[80,16]{0,1:T(8,128)(4,1)S(1)}, pred[80,16]{0,1:T(8,128)(4,1)}, u32[]{:S(2)}) copy-start(pred[80,16]{0,1:T(8,128)(4,1)} %fusion.167) | copy-start | bytes 3844
  973.9 40.9 %copy-start.96 = (s32[64]{0:T(128)S(1)}, s32[64]{0:T(128)}, u32[]{:S(2)}) copy-start(s32[64]{0:T(128)} %copy-done.95) | copy-start | bytes 772
  973.9 40.9 %copy-start.102 = (s32[64,1]{0,1:T(1,128)S(1)}, s32[64,1]{0,1:T(1,128)}, u32[]{:S(2)}) copy-start(s32[64,1]{0,1:T(1,128)} %mul.1176) | copy-start | bytes 772
  973.9 40.9 %copy-start.101 = (s32[3]{0:T(128)S(1)}, s32[3]{0:T(128)}, u32[]{:S(2)}) copy-start(s32[3]{0:T(128)} %constant.435.clone.1) | copy-start | bytes 40
  974.5 52.3 %copy-start.103 = (bf16[1,1,2,1536,256]{4,3,2,1,0:T(8,128)(2,1)S(1)}, bf16[1,1,2,1536,256]{4,3,2,1,0:T(8,128)(2,1)}, u32[]{:S(2)}) copy-start(bf16[1,1,2,1536,256]{4,3,2,1,0:T(8,128)(2,1)} %param.58) | copy-start | bytes 4718596
  1010.8 15.8 %all-to-all-start.10 = ((bf16[16,5,1536]{2,1,0:T(8,128)(2,1)}), bf16[16,5,1536]{2,1,0:T(8,128)(2,1)S(1)}, u32[]{:S(2)}, u32[]{:S(2)}) async-start(bf16[16,5,1536]{2,1,0:T(8,128)(2,1)} %reshape.3028), calls=%async_computation.10 | async-start | bytes 786432 | tf_op jit(solution)/shard_map/all_to_all | solution.py:177
  1014.7 106.9 %all-reduce.17.cloned.1.call-start = ((), (), s32[]{:S(2)}) async-start(), calls=%async_computation.17 | async-start | bytes 491520 | tf_op jit(solution)/shard_map/psum | solution.py:187
  1027.2 102.7 %copy-start.106 = (bf16[1,1536,16]{1,2,0:T(8,128)(2,1)S(1)}, bf16[1,1536,16]{1,2,0:T(8,128)(2,1)}, u32[]{:S(2)}) copy-start(bf16[1,1536,16]{1,2,0:T(8,128)(2,1)} %param.57) | copy-start | bytes 147460
  1027.3 102.9 %copy-start.45 = (s32[1,1,16,4]{2,3,1,0:T(4,128)S(1)}, s32[1,1,16,4]{2,3,1,0:T(4,128)}, u32[]{:S(2)}) copy-start(s32[1,1,16,4]{2,3,1,0:T(4,128)} %get-tuple-element.215) | copy-start | bytes 772
  1123.4 19.0 %all-to-all-start.11 = ((bf16[16,5,1536]{2,1,0:T(8,128)(2,1)}), bf16[16,5,1536]{2,1,0:T(8,128)(2,1)S(1)}, u32[]{:S(2)}, u32[]{:S(2)}) async-start(bf16[16,5,1536]{2,1,0:T(8,128)(2,1)} %copy.316), calls=%async_computation.11 | async-start | bytes 786432 | tf_op jit(solution)/shard_map/all_to_all | solution.py:188
  (73 other events, 743.8 us)
Sparse Core Ops, SparseCore 0:
  102.0 98.1 all-reduce.6
  293.8 94.1 all-reduce.8
  479.0 93.1 all-reduce.10
  663.2 93.2 all-reduce.12
  847.4 93.1 all-reduce.14
  1028.4 93.1 all-reduce.16
where the time goes:
time: 1160 us; the launch traced here: 1150 us
  waiting for transfers between devices  686 us (59%)
  blocking collectives  214 us (18%)
  starting transfers between devices  90.3 us (8%)
  other arithmetic  52.8 us (5%)
  local copies, waits for them, and re-layouts  50.7 us (4%)
  matrix products  41.9 us (4%)
  between operations  16.2 us (1%)
    psum x6, waiting for transfers between devices, local(): summed = lax.psum(partial_out.astype(jnp.bfloat16), 'expert')  560 us
    psum x6, blocking collectives, local(): lax.psum(jnp.dot(attended, out_weight, preferred_element_type=jnp.float32...  214 us
    all_to_all x6, waiting for transfers between devices, local(): lax.all_to_all(outbound, 'replica', split_axis=0, concat_axis=0, tiled=True)  59.6 us
    all_to_all x6, waiting for transfers between devices, local(): lax.all_to_all(summed, 'replica', split_axis=0, concat_axis=0, tiled=True)  56.2 us
    all_to_all x6, starting transfers between devices, local(): lax.all_to_all(summed, 'replica', split_axis=0, concat_axis=0, tiled=True)  39.2 us
  transfers between devices with their start and end apart: 25, of which 24 were waited for; matrix products, arithmetic and copies ran while one was open for 4% of the time, Pallas kernels for 0%

commit v1 on v0

--- a/solution.py
+++ b/solution.py
@@ -184,7 +184,7 @@
         partial_out = jnp.dot(hidden, down_weight, preferred_element_type=jnp.float32).reshape(
             source_count, slot_count, model_width
         )
-        summed = lax.psum(partial_out.astype(jnp.bfloat16), "expert")
+        summed = jnp.sum(lax.all_gather(partial_out.astype(jnp.bfloat16), "expert"), axis=0)
         returned = lax.all_to_all(summed, "replica", split_axis=0, concat_axis=0, tiled=True)
         picked = returned.reshape(expert_count * slot_cap, model_width)[target]
         picked = picked.reshape(row_count, choose_count, model_width).astype(jnp.float32)

time: 1160 us -> 921 us (0.79)
  waiting for transfers between devices: 686 us -> 419 us
  blocking collectives: 214 us -> 304 us
  starting transfers between devices: 90.3 us -> 56.6 us
  local copies, waits for them, and re-layouts: 50.7 us -> 28.2 us
    psum x6 -> x0, waiting for transfers between devices: 560 us -> none  [local(): summed = lax.psum(partial_out.astype(jnp.bfloat16), 'expert')]
    all_gather x0 -> x6, waiting for transfers between devices: none -> 349 us  [local(): lax.all_gather(partial_out.astype(jnp.bfloat16), 'expert')]
    all_to_all x0 -> x6, blocking collectives: none -> 80.4 us  [local(): lax.all_to_all(outbound, 'replica', split_axis=0, concat_axis=0, tiled=True)]
    all_to_all x6 -> x0, waiting for transfers between devices: 59.6 us -> none  [local(): lax.all_to_all(outbound, 'replica', split_axis=0, concat_axis=0, tiled=True)]
    all_to_all x6 -> x0, starting transfers between devices: 22.9 us -> none  [local(): lax.all_to_all(outbound, 'replica', split_axis=0, concat_axis=0, tiled=True)]
  transfers between devices with their start and end apart: 25 -> 19, of which waited for: 24 -> 18; matrix products, arithmetic and copies ran while one was open for 4% -> 4% of each run, Pallas kernels for 0% -> 0%
where the time goes in v1:
time: 921 us; the launch traced here: 918 us
  waiting for transfers between devices  419 us (45%)
  blocking collectives  304 us (33%)
  starting transfers between devices  56.6 us (6%)
  other arithmetic  54.1 us (6%)
  matrix products  39.5 us (4%)
  local copies, waits for them, and re-layouts  28.2 us (3%)
  between operations  16.8 us (2%)
    all_gather x6, waiting for transfers between devices, local(): lax.all_gather(partial_out.astype(jnp.bfloat16), 'expert')  349 us
    psum x6, blocking collectives, local(): lax.psum(jnp.dot(attended, out_weight, preferred_element_type=jnp.float32...  223 us
    all_to_all x6, blocking collectives, local(): lax.all_to_all(outbound, 'replica', split_axis=0, concat_axis=0, tiled=True)  80.4 us
    all_to_all x6, waiting for transfers between devices, local(): lax.all_to_all(summed, 'replica', split_axis=0, concat_axis=0, tiled=True)  58.2 us
    all_to_all x6, starting transfers between devices, local(): lax.all_to_all(summed, 'replica', split_axis=0, concat_axis=0, tiled=True)  29.1 us
  transfers between devices with their start and end apart: 19, of which 18 were waited for; matrix products, arithmetic and copies ran while one was open for 4% of the time, Pallas kernels for 0%

profile of v1, /device:TPU:1, one launch (start us, length us, event | category | flops | bytes accessed | tf_op | source)
XLA Modules:
  0.0 918.1 jit_solution(3386102499760962637)
XLA Ops:
  8.1 9.5 %collective-permute-start = (s32[4,8]{0,1:T(8,128)S(1)}, s32[4,8]{0,1:T(8,128)S(1)}, u32[]{:S(2)}, u32[]{:S(2)}) collective-permute-start(s32[4,8]{0,1:T(8,128)S(1)} %slice.535), channel_id=1, source_target_pairs={{0,120},{8,0},{16,8},{24,16},{32,24},{40,32},{48,40},{56,48},{64,5... | collective-permute-start | bytes 392 | tf_op jit(solution)/shard_map/ppermute | solution.py:14
  17.7 1.3 iota_compare_fusion.18
  19.7 1.5 broadcast_multiply_fusion
  22.7 1.5 copy.319
  29.5 1.9 collective-permute-start.1
  32.2 7.0 collective-permute-done.1
  42.4 38.7 %psum.42 = bf16[16,1536]{1,0:T(8,128)(2,1)S(1)} all-reduce(bf16[16,1536]{1,0:T(8,128)(2,1)S(1)} %convolution_convert_fusion.17), channel_id=1, replica_groups=mesh['section'=4,'replica'=16,'expert'=8] {'expert'}, use_global_device_ids=true, to_apply=%region_7.8 | all-reduce | flops 24576 | bytes 98304 | tf_op jit(solution)/shard_map/psum | solution.py:157
  82.0 12.6 %all_to_all.60 = bf16[16,5,1536]{2,1,0:T(8,128)(2,1)S(1)} all-to-all(bf16[16,5,1536]{2,1,0:T(8,128)(2,1)S(1)} %reshape.2989), channel_id=1, replica_groups=mesh['section'=4,'replica'=16,'expert'=8] {'replica'}, dimensions={0} | all-to-all | bytes 491520 | tf_op jit(solution)/shard_map/all_to_all | solution.py:177
  94.7 1.4 fusion.46
  96.1 1.4 fusion
  100.1 61.3 %all-gather.13.cloned.1.call-done = bf16[128,5,1536]{2,0,1:T(8,128)(2,1)} async-done(((bf16[16,5,1536]{2,0,1:T(8,128)(2,1)}), bf16[128,5,1536]{2,0,1:T(8,128)(2,1)}) %all-gather.13.cloned.1.call-update) | async-done | bytes 1966096 | tf_op jit(solution)/shard_map/all_gather | solution.py:187
  161.5 1.9 reduce_sum.536
  164.3 4.8 all-to-all-start.1
  170.9 10.2 %all-to-all-done.1 = bf16[16,5,1536]{2,1,0:T(8,128)(2,1)S(1)} async-done(((bf16[16,5,1536]{2,1,0:T(8,128)(2,1)}), bf16[16,5,1536]{2,1,0:T(8,128)(2,1)S(1)}, u32[]{:S(2)}, u32[]{:S(2)}) %all-to-all-start.1) | async-done | bytes 245792 | tf_op jit(solution)/shard_map/all_to_all | solution.py:188
  182.5 3.2 collective-permute-start.2
  185.8 1.1 collective-permute-done.2
  193.5 36.9 %psum.43 = bf16[16,1536]{1,0:T(8,128)(2,1)S(1)} all-reduce(bf16[16,1536]{1,0:T(8,128)(2,1)S(1)} %convolution_convert_fusion.16), channel_id=1, replica_groups=mesh['section'=4,'replica'=16,'expert'=8] {'expert'}, use_global_device_ids=true, to_apply=%region_23.24 | all-reduce | flops 24576 | bytes 98304 | tf_op jit(solution)/shard_map/psum | solution.py:157
  231.2 13.5 %all_to_all.61 = bf16[16,5,1536]{2,1,0:T(8,128)(2,1)S(1)} all-to-all(bf16[16,5,1536]{2,1,0:T(8,128)(2,1)S(1)} %reshape.2996), channel_id=1, replica_groups=mesh['section'=4,'replica'=16,'expert'=8] {'replica'}, dimensions={0} | all-to-all | bytes 491520 | tf_op jit(solution)/shard_map/all_to_all | solution.py:177
  244.9 1.4 fusion.44
  246.3 1.4 fusion.1
  249.7 58.9 %all-gather.15.cloned.1.call-done = bf16[128,5,1536]{2,0,1:T(8,128)(2,1)} async-done(((bf16[16,5,1536]{2,0,1:T(8,128)(2,1)}), bf16[128,5,1536]{2,0,1:T(8,128)(2,1)}) %all-gather.15.cloned.1.call-update) | async-done | bytes 1966096 | tf_op jit(solution)/shard_map/all_gather | solution.py:187
  308.6 1.9 reduce_sum.547
  311.4 4.8 all-to-all-start.3
  319.4 8.9 all-to-all-done.3
  329.7 3.3 collective-permute-start.3
  338.7 36.9 %psum.44 = bf16[16,1536]{1,0:T(8,128)(2,1)S(1)} all-reduce(bf16[16,1536]{1,0:T(8,128)(2,1)S(1)} %convolution_convert_fusion.15), channel_id=1, replica_groups=mesh['section'=4,'replica'=16,'expert'=8] {'expert'}, use_global_device_ids=true, to_apply=%region_39.40 | all-reduce | flops 24576 | bytes 98304 | tf_op jit(solution)/shard_map/psum | solution.py:157
  376.4 13.6 %all_to_all.62 = bf16[16,5,1536]{2,1,0:T(8,128)(2,1)S(1)} all-to-all(bf16[16,5,1536]{2,1,0:T(8,128)(2,1)S(1)} %reshape.3004), channel_id=1, replica_groups=mesh['section'=4,'replica'=16,'expert'=8] {'replica'}, dimensions={0} | all-to-all | bytes 491520 | tf_op jit(solution)/shard_map/all_to_all | solution.py:177
  390.1 1.4 fusion.42
  391.5 1.4 fusion.2
  394.9 58.9 %all-gather.17.cloned.1.call-done = bf16[128,5,1536]{2,0,1:T(8,128)(2,1)} async-done(((bf16[16,5,1536]{2,0,1:T(8,128)(2,1)}), bf16[128,5,1536]{2,0,1:T(8,128)(2,1)}) %all-gather.17.cloned.1.call-update) | async-done | bytes 1966096 | tf_op jit(solution)/shard_map/all_gather | solution.py:187
  453.8 1.9 reduce_sum.558
  456.6 4.8 all-to-all-start.5
  463.8 9.6 %all-to-all-done.5 = bf16[16,5,1536]{2,1,0:T(8,128)(2,1)S(1)} async-done(((bf16[16,5,1536]{2,1,0:T(8,128)(2,1)}), bf16[16,5,1536]{2,1,0:T(8,128)(2,1)S(1)}, u32[]{:S(2)}, u32[]{:S(2)}) %all-to-all-start.5) | async-done | bytes 245792 | tf_op jit(solution)/shard_map/all_to_all | solution.py:188
  474.9 3.1 collective-permute-start.4
  483.7 36.9 %psum.45 = bf16[16,1536]{1,0:T(8,128)(2,1)S(1)} all-reduce(bf16[16,1536]{1,0:T(8,128)(2,1)S(1)} %convolution_convert_fusion.14), channel_id=1, replica_groups=mesh['section'=4,'replica'=16,'expert'=8] {'expert'}, use_global_device_ids=true, to_apply=%region_55.56 | all-reduce | flops 24576 | bytes 98304 | tf_op jit(solution)/shard_map/psum | solution.py:157
  521.7 13.6 %all_to_all.63 = bf16[16,5,1536]{2,1,0:T(8,128)(2,1)S(1)} all-to-all(bf16[16,5,1536]{2,1,0:T(8,128)(2,1)S(1)} %reshape.3012), channel_id=1, replica_groups=mesh['section'=4,'replica'=16,'expert'=8] {'replica'}, dimensions={0} | all-to-all | bytes 491520 | tf_op jit(solution)/shard_map/all_to_all | solution.py:177
  535.4 1.4 fusion.40
  536.8 1.4 fusion.3
  540.2 58.9 %all-gather.19.cloned.1.call-done = bf16[128,5,1536]{2,0,1:T(8,128)(2,1)} async-done(((bf16[16,5,1536]{2,0,1:T(8,128)(2,1)}), bf16[128,5,1536]{2,0,1:T(8,128)(2,1)}) %all-gather.19.cloned.1.call-update) | async-done | bytes 1966096 | tf_op jit(solution)/shard_map/all_gather | solution.py:187
  599.1 1.9 reduce_sum.569
  601.9 4.8 all-to-all-start.7
  609.9 8.9 all-to-all-done.7
  620.2 3.1 collective-permute-start.5
  629.1 36.9 %psum.46 = bf16[16,1536]{1,0:T(8,128)(2,1)S(1)} all-reduce(bf16[16,1536]{1,0:T(8,128)(2,1)S(1)} %convolution_convert_fusion.13), channel_id=1, replica_groups=mesh['section'=4,'replica'=16,'expert'=8] {'expert'}, use_global_device_ids=true, to_apply=%region_71.72 | all-reduce | flops 24576 | bytes 98304 | tf_op jit(solution)/shard_map/psum | solution.py:157
  666.9 13.5 %all_to_all.64 = bf16[16,5,1536]{2,1,0:T(8,128)(2,1)S(1)} all-to-all(bf16[16,5,1536]{2,1,0:T(8,128)(2,1)S(1)} %reshape.3020), channel_id=1, replica_groups=mesh['section'=4,'replica'=16,'expert'=8] {'replica'}, dimensions={0} | all-to-all | bytes 491520 | tf_op jit(solution)/shard_map/all_to_all | solution.py:177
  680.5 1.4 fusion.38
  682.0 1.4 fusion.4
  685.3 58.9 %all-gather.21.cloned.1.call-done = bf16[128,5,1536]{2,0,1:T(8,128)(2,1)} async-done(((bf16[16,5,1536]{2,0,1:T(8,128)(2,1)}), bf16[128,5,1536]{2,0,1:T(8,128)(2,1)}) %all-gather.21.cloned.1.call-update) | async-done | bytes 1966096 | tf_op jit(solution)/shard_map/all_gather | solution.py:187
  744.2 1.9 reduce_sum.580
  747.0 4.8 all-to-all-start.9
  754.3 9.6 %all-to-all-done.9 = bf16[16,5,1536]{2,1,0:T(8,128)(2,1)S(1)} async-done(((bf16[16,5,1536]{2,1,0:T(8,128)(2,1)}), bf16[16,5,1536]{2,1,0:T(8,128)(2,1)S(1)}, u32[]{:S(2)}, u32[]{:S(2)}) %all-to-all-start.9) | async-done | bytes 245792 | tf_op jit(solution)/shard_map/all_to_all | solution.py:188
  765.3 3.1 collective-permute-start.6
  774.3 36.9 %psum.47 = bf16[16,1536]{1,0:T(8,128)(2,1)S(1)} all-reduce(bf16[16,1536]{1,0:T(8,128)(2,1)S(1)} %convolution_convert_fusion.12), channel_id=1, replica_groups=mesh['section'=4,'replica'=16,'expert'=8] {'expert'}, use_global_device_ids=true, to_apply=%region_87.88 | all-reduce | flops 24576 | bytes 98304 | tf_op jit(solution)/shard_map/psum | solution.py:157
  811.7 13.5 %all_to_all.65 = bf16[16,5,1536]{2,1,0:T(8,128)(2,1)S(1)} all-to-all(bf16[16,5,1536]{2,1,0:T(8,128)(2,1)S(1)} %reshape.3028), channel_id=1, replica_groups=mesh['section'=4,'replica'=16,'expert'=8] {'replica'}, dimensions={0} | all-to-all | bytes 491520 | tf_op jit(solution)/shard_map/all_to_all | solution.py:177
  825.4 1.4 fusion.36
  826.8 1.4 fusion.5
  831.0 1.3 constant_dynamic-update-slice_fusion.10
  832.3 1.4 select_select_fusion.4
  833.7 1.4 select_select_fusion.3
  835.1 1.4 select_select_fusion.2
  837.3 51.7 %all-gather.23.cloned.1.call-done = bf16[128,5,1536]{2,0,1:T(8,128)(2,1)} async-done(((bf16[16,5,1536]{2,0,1:T(8,128)(2,1)}), bf16[128,5,1536]{2,0,1:T(8,128)(2,1)}) %all-gather.23.cloned.1.call-update) | async-done | bytes 1966096 | tf_op jit(solution)/shard_map/all_gather | solution.py:187
  889.0 1.9 reduce_sum.591
  891.8 4.8 all-to-all-start.11
  897.8 10.9 %all-to-all-done.11 = bf16[16,5,1536]{2,1,0:T(8,128)(2,1)S(1)} async-done(((bf16[16,5,1536]{2,1,0:T(8,128)(2,1)}), bf16[16,5,1536]{2,1,0:T(8,128)(2,1)S(1)}, u32[]{:S(2)}, u32[]{:S(2)}) %all-to-all-start.11) | async-done | bytes 245792 | tf_op jit(solution)/shard_map/all_to_all | solution.py:188
  (655 shorter events, 88.5 us)
Async XLA Ops:
  7.2 90.4 %copy-start = (bf16[1,1,256,1536]{3,2,1,0:T(8,128)(2,1)S(1)}, bf16[1,1,256,1536]{3,2,1,0:T(8,128)(2,1)}, u32[]{:S(2)}) copy-start(bf16[1,1,256,1536]{3,2,1,0:T(8,128)(2,1)} %param.59) | copy-start | bytes 2359300
  7.2 17.0 %copy-start.3 = (bf16[3,16,1536]{2,1,0:T(8,128)(2,1)S(1)}, bf16[3,16,1536]{2,1,0:T(8,128)(2,1)}, u32[]{:S(2)}) copy-start(bf16[3,16,1536]{2,1,0:T(8,128)(2,1)} %param.50) | copy-start | bytes 442372
  7.2 17.2 %copy-start.92 = (f32[1,1536]{1,0:T(1,128)S(1)}, f32[1,1536]{1,0:T(1,128)}, u32[]{:S(2)}) copy-start(f32[1,1536]{1,0:T(1,128)} %param.51) | copy-start | bytes 18436
  7.2 17.6 %copy-start.2 = (bf16[1,1536,1,128]{3,1,2,0:T(8,128)(2,1)S(1)}, bf16[1,1536,1,128]{3,1,2,0:T(8,128)(2,1)}, u32[]{:S(2)}) copy-start(bf16[1,1536,1,128]{3,1,2,0:T(8,128)(2,1)} %param.53) | copy-start | bytes 1179652
  7.2 154.3 %all-gather.13.cloned.1.call-start = ((), (), s32[]{:S(2)}) async-start(), calls=%async_computation.12 | async-start | bytes 2211840 | tf_op jit(solution)/shard_map/all_gather | solution.py:187
  8.1 20.6 %collective-permute-start = (s32[4,8]{0,1:T(8,128)S(1)}, s32[4,8]{0,1:T(8,128)S(1)}, u32[]{:S(2)}, u32[]{:S(2)}) collective-permute-start(s32[4,8]{0,1:T(8,128)S(1)} %slice.535), channel_id=1, source_target_pairs={{0,120},{8,0},{16,8},{24,16},{32,24},{40,32},{48,40},{56,48},{64,5... | collective-permute-start | bytes 392 | tf_op jit(solution)/shard_map/ppermute | solution.py:14
  17.7 9.2 %copy-start.74 = (f32[32]{0:T(128)}, f32[32]{0:T(128)S(1)}, u32[]{:S(2)}) copy-start(f32[32]{0:T(128)S(1)} %multiply_power_fusion) | copy-start | bytes 388
  26.8 14.5 %copy-start.21 = (bf16[3,16,1,128]{3,1,2,0:T(8,128)(2,1)}, bf16[3,16,1,128]{3,1,2,0:T(8,128)(2,1)S(1)}, u32[]{:S(2)}) copy-start(bf16[3,16,1,128]{3,1,2,0:T(8,128)(2,1)S(1)} %constant_dynamic-update-slice_fusion.11) | copy-start | bytes 36868
  26.9 14.4 %copy-start.39 = (f32[1,4]{1,0:T(1,128)S(1)}, f32[1,4]{1,0:T(1,128)}, u32[]{:S(2)}) copy-start(f32[1,4]{1,0:T(1,128)} %param.54) | copy-start | bytes 52
  29.5 9.7 %collective-permute-start.1 = (bf16[32,16,1,128]{3,1,0,2:T(8,128)(2,1)S(1)}, bf16[32,16,1,128]{3,1,0,2:T(8,128)(2,1)}, u32[]{:S(2)}, u32[]{:S(2)}) collective-permute-start(bf16[32,16,1,128]{3,1,0,2:T(8,128)(2,1)S(1)} %bitcast.429), channel_id=1, source_target_pairs={{0,8},{8,16},{16,24},{24,32},{32,40},{40,48},{48,56},{56,64},{64,7... | collective-permute-start | bytes 393224 | tf_op jit(solution)/shard_map/ppermute | solution.py:14
  32.1 10.1 %copy-start.1 = (bf16[1,256,1536]{2,1,0:T(8,128)(2,1)S(1)}, bf16[1,256,1536]{2,1,0:T(8,128)(2,1)}, u32[]{:S(2)}) copy-start(bf16[1,256,1536]{2,1,0:T(8,128)(2,1)} %param.55) | copy-start | bytes 2359300
  32.1 9.1 copy-start.85
  99.3 62.2 %copy-start.114 = (s32[64]{0:T(128)}, s32[64]{0:T(128)S(1)}, u32[]{:S(2)}) copy-start(s32[64]{0:T(128)S(1)} %select_reduce_fusion.8) | copy-start | bytes 772
  161.5 8.4 copy-start.20
  161.5 8.4 copy-start.128
  161.5 8.5 copy-start.73
  164.3 16.9 %all-to-all-start.1 = ((bf16[16,5,1536]{2,1,0:T(8,128)(2,1)}), bf16[16,5,1536]{2,1,0:T(8,128)(2,1)S(1)}, u32[]{:S(2)}, u32[]{:S(2)}) async-start(bf16[16,5,1536]{2,1,0:T(8,128)(2,1)} %copy.333), calls=%async_computation.1 | async-start | bytes 786432 | tf_op jit(solution)/shard_map/all_to_all | solution.py:188
  169.1 139.4 %all-gather.15.cloned.1.call-start = ((), (), s32[]{:S(2)}) async-start(), calls=%async_computation.13 | async-start | bytes 2211840 | tf_op jit(solution)/shard_map/all_gather | solution.py:187
  182.2 9.2 %copy-start.24 = (bf16[3,16,1,128]{3,1,2,0:T(8,128)(2,1)S(1)}, bf16[3,16,1,128]{3,1,2,0:T(8,128)(2,1)}, u32[]{:S(2)}) copy-start(bf16[3,16,1,128]{3,1,2,0:T(8,128)(2,1)} %broadcast_select_fusion.4) | copy-start | bytes 36868
  182.2 10.2 %copy-start.40 = (f32[1,4]{1,0:T(1,128)S(1)}, f32[1,4]{1,0:T(1,128)}, u32[]{:S(2)}) copy-start(f32[1,4]{1,0:T(1,128)} %param.54) | copy-start | bytes 52
  182.5 4.4 collective-permute-start.2
  190.3 40.3 %copy-start.80 = (pred[80,16]{0,1:T(8,128)(4,1)S(1)}, pred[80,16]{0,1:T(8,128)(4,1)}, u32[]{:S(2)}) copy-start(pred[80,16]{0,1:T(8,128)(4,1)} %fusion.163) | copy-start | bytes 3844
  192.1 38.4 %copy-start.25 = (bf16[3,16,1,128]{3,1,2,0:T(8,128)(2,1)}, bf16[3,16,1,128]{3,1,2,0:T(8,128)(2,1)S(1)}, u32[]{:S(2)}) copy-start(bf16[3,16,1,128]{3,1,2,0:T(8,128)(2,1)S(1)} %constant_dynamic-update-slice_fusion.9) | copy-start | bytes 36868
  249.5 59.1 %copy-start.110 = (s32[64]{0:T(128)}, s32[64]{0:T(128)S(1)}, u32[]{:S(2)}) copy-start(s32[64]{0:T(128)S(1)} %select_reduce_fusion.6) | copy-start | bytes 772
  308.6 9.7 %copy-start.14 = (bf16[16,1536]{1,0:T(8,128)(2,1)S(1)}, bf16[16,1536]{1,0:T(8,128)(2,1)}, u32[]{:S(2)}) copy-start(bf16[16,1536]{1,0:T(8,128)(2,1)} %copy-done.13) | copy-start | bytes 147460
  308.6 9.7 %copy-start.126 = (f32[16]{0:T(128)S(1)}, f32[16]{0:T(128)}, u32[]{:S(2)}) copy-start(f32[16]{0:T(128)} %copy-done.125) | copy-start | bytes 196
  308.6 9.7 %copy-start.134 = (bf16[1,1536,16]{1,2,0:T(8,128)(2,1)S(1)}, bf16[1,1536,16]{1,2,0:T(8,128)(2,1)}, u32[]{:S(2)}) copy-start(bf16[1,1536,16]{1,2,0:T(8,128)(2,1)} %param.57) | copy-start | bytes 147460
  308.6 9.8 %copy-start.71 = (s32[1,1,16,4]{2,3,1,0:T(4,128)S(1)}, s32[1,1,16,4]{2,3,1,0:T(4,128)}, u32[]{:S(2)}) copy-start(s32[1,1,16,4]{2,3,1,0:T(4,128)} %get-tuple-element.291) | copy-start | bytes 772
  311.4 16.9 %all-to-all-start.3 = ((bf16[16,5,1536]{2,1,0:T(8,128)(2,1)}), bf16[16,5,1536]{2,1,0:T(8,128)(2,1)S(1)}, u32[]{:S(2)}, u32[]{:S(2)}) async-start(bf16[16,5,1536]{2,1,0:T(8,128)(2,1)} %copy.344), calls=%async_computation.3 | async-start | bytes 786432 | tf_op jit(solution)/shard_map/all_to_all | solution.py:188
  316.3 137.5 %all-gather.17.cloned.1.call-start = ((), (), s32[]{:S(2)}) async-start(), calls=%async_computation.14 | async-start | bytes 2211840 | tf_op jit(solution)/shard_map/all_gather | solution.py:187
  329.7 8.4 copy-start.46
  329.7 4.3 collective-permute-start.3
  336.0 39.7 %copy-start.83 = (pred[80,16]{0,1:T(8,128)(4,1)S(1)}, pred[80,16]{0,1:T(8,128)(4,1)}, u32[]{:S(2)}) copy-start(pred[80,16]{0,1:T(8,128)(4,1)} %fusion.164) | copy-start | bytes 3844
  337.3 38.5 %copy-start.29 = (bf16[3,16,1,128]{3,1,2,0:T(8,128)(2,1)}, bf16[3,16,1,128]{3,1,2,0:T(8,128)(2,1)S(1)}, u32[]{:S(2)}) copy-start(bf16[3,16,1,128]{3,1,2,0:T(8,128)(2,1)S(1)} %constant_dynamic-update-slice_fusion.7) | copy-start | bytes 36868
  394.7 61.9 %copy-start.112 = (s32[64]{0:T(128)}, s32[64]{0:T(128)S(1)}, u32[]{:S(2)}) copy-start(s32[64]{0:T(128)S(1)} %select_reduce_fusion.4) | copy-start | bytes 772
  453.8 8.9 copy-start.16
  453.8 8.9 copy-start.130
  453.8 8.9 copy-start.135
  453.8 9.1 copy-start.69
  456.6 16.9 %all-to-all-start.5 = ((bf16[16,5,1536]{2,1,0:T(8,128)(2,1)}), bf16[16,5,1536]{2,1,0:T(8,128)(2,1)S(1)}, u32[]{:S(2)}, u32[]{:S(2)}) async-start(bf16[16,5,1536]{2,1,0:T(8,128)(2,1)} %copy.355), calls=%async_computation.5 | async-start | bytes 786432 | tf_op jit(solution)/shard_map/all_to_all | solution.py:188
  461.4 137.7 %all-gather.19.cloned.1.call-start = ((), (), s32[]{:S(2)}) async-start(), calls=%async_computation.15 | async-start | bytes 2211840 | tf_op jit(solution)/shard_map/all_gather | solution.py:187
  474.9 4.3 collective-permute-start.4
  481.2 40.2 %copy-start.82 = (pred[80,16]{0,1:T(8,128)(4,1)S(1)}, pred[80,16]{0,1:T(8,128)(4,1)}, u32[]{:S(2)}) copy-start(pred[80,16]{0,1:T(8,128)(4,1)} %fusion.165) | copy-start | bytes 3844
  482.4 38.5 %copy-start.27 = (bf16[3,16,1,128]{3,1,2,0:T(8,128)(2,1)}, bf16[3,16,1,128]{3,1,2,0:T(8,128)(2,1)S(1)}, u32[]{:S(2)}) copy-start(bf16[3,16,1,128]{3,1,2,0:T(8,128)(2,1)S(1)} %constant_dynamic-update-slice_fusion.5) | copy-start | bytes 36868
  540.0 59.1 %copy-start.108 = (s32[64]{0:T(128)}, s32[64]{0:T(128)S(1)}, u32[]{:S(2)}) copy-start(s32[64]{0:T(128)S(1)} %select_reduce_fusion.2) | copy-start | bytes 772
  599.1 9.7 %copy-start.12 = (bf16[16,1536]{1,0:T(8,128)(2,1)S(1)}, bf16[16,1536]{1,0:T(8,128)(2,1)}, u32[]{:S(2)}) copy-start(bf16[16,1536]{1,0:T(8,128)(2,1)} %copy-done.11) | copy-start | bytes 147460
  599.1 9.7 %copy-start.124 = (f32[16]{0:T(128)S(1)}, f32[16]{0:T(128)}, u32[]{:S(2)}) copy-start(f32[16]{0:T(128)} %copy-done.123) | copy-start | bytes 196
  599.1 9.7 %copy-start.136 = (bf16[1,1536,16]{1,2,0:T(8,128)(2,1)S(1)}, bf16[1,1536,16]{1,2,0:T(8,128)(2,1)}, u32[]{:S(2)}) copy-start(bf16[1,1536,16]{1,2,0:T(8,128)(2,1)} %param.57) | copy-start | bytes 147460
  599.1 9.8 %copy-start.67 = (s32[1,1,16,4]{2,3,1,0:T(4,128)S(1)}, s32[1,1,16,4]{2,3,1,0:T(4,128)}, u32[]{:S(2)}) copy-start(s32[1,1,16,4]{2,3,1,0:T(4,128)} %get-tuple-element.287) | copy-start | bytes 772
  601.9 16.9 %all-to-all-start.7 = ((bf16[16,5,1536]{2,1,0:T(8,128)(2,1)}), bf16[16,5,1536]{2,1,0:T(8,128)(2,1)S(1)}, u32[]{:S(2)}, u32[]{:S(2)}) async-start(bf16[16,5,1536]{2,1,0:T(8,128)(2,1)} %copy.366), calls=%async_computation.7 | async-start | bytes 786432 | tf_op jit(solution)/shard_map/all_to_all | solution.py:188
  606.8 137.4 %all-gather.21.cloned.1.call-start = ((), (), s32[]{:S(2)}) async-start(), calls=%async_computation.16 | async-start | bytes 2211840 | tf_op jit(solution)/shard_map/all_gather | solution.py:187
  620.2 4.3 collective-permute-start.5
  626.5 39.7 %copy-start.84 = (pred[80,16]{0,1:T(8,128)(4,1)S(1)}, pred[80,16]{0,1:T(8,128)(4,1)}, u32[]{:S(2)}) copy-start(pred[80,16]{0,1:T(8,128)(4,1)} %fusion.166) | copy-start | bytes 3844
  627.7 38.5 %copy-start.31 = (bf16[3,16,1,128]{3,1,2,0:T(8,128)(2,1)}, bf16[3,16,1,128]{3,1,2,0:T(8,128)(2,1)S(1)}, u32[]{:S(2)}) copy-start(bf16[3,16,1,128]{3,1,2,0:T(8,128)(2,1)S(1)} %constant_dynamic-update-slice_fusion.3) | copy-start | bytes 36868
  685.1 59.1 %copy-start.106 = (s32[64]{0:T(128)}, s32[64]{0:T(128)S(1)}, u32[]{:S(2)}) copy-start(s32[64]{0:T(128)S(1)} %select_reduce_fusion) | copy-start | bytes 772
  744.2 9.0 copy-start.18
  744.2 9.0 copy-start.132
  744.2 9.0 copy-start.137
  744.2 9.2 copy-start.65
  747.0 16.9 %all-to-all-start.9 = ((bf16[16,5,1536]{2,1,0:T(8,128)(2,1)}), bf16[16,5,1536]{2,1,0:T(8,128)(2,1)S(1)}, u32[]{:S(2)}, u32[]{:S(2)}) async-start(bf16[16,5,1536]{2,1,0:T(8,128)(2,1)} %copy.377), calls=%async_computation.9 | async-start | bytes 786432 | tf_op jit(solution)/shard_map/all_to_all | solution.py:188
  751.9 137.1 %all-gather.23.cloned.1.call-start = ((), (), s32[]{:S(2)}) async-start(), calls=%async_computation.17 | async-start | bytes 2211840 | tf_op jit(solution)/shard_map/all_gather | solution.py:187
  765.3 4.3 collective-permute-start.6
  771.6 39.7 %copy-start.81 = (pred[80,16]{0,1:T(8,128)(4,1)S(1)}, pred[80,16]{0,1:T(8,128)(4,1)}, u32[]{:S(2)}) copy-start(pred[80,16]{0,1:T(8,128)(4,1)} %fusion.167) | copy-start | bytes 3844
  891.8 16.9 %all-to-all-start.11 = ((bf16[16,5,1536]{2,1,0:T(8,128)(2,1)}), bf16[16,5,1536]{2,1,0:T(8,128)(2,1)S(1)}, u32[]{:S(2)}, u32[]{:S(2)}) async-start(bf16[16,5,1536]{2,1,0:T(8,128)(2,1)} %copy.388), calls=%async_computation.11 | async-start | bytes 786432 | tf_op jit(solution)/shard_map/all_to_all | solution.py:188
  (98 other events, 472.0 us)
Sparse Core Ops, SparseCore 0:
  98.7 62.7 all-gather.12
  248.9 59.6 all-gather.14
  394.1 59.6 all-gather.16
  539.4 59.6 all-gather.18
  684.5 59.6 all-gather.20
  829.3 59.6 all-gather.22
